TPU v7x, 768 devices: a whole 4x8x12 slice. The times are simulated.
768 devices in a mesh: mem: 48 (over x, z), ctx: 8 (over y), dp: 2 (over core).
Axes of the slice: x: 4, y: 8, z: 12, core: 2. Of those that a mesh axis runs over, the one named last changes fastest.
Arguments:
- queries: bfloat16 [2, 49152, 32, 128], P('dp', ('mem', 'ctx')), may hold values from -6 to 6
- window_keys: bfloat16 [2, 49152, 32, 128], P('dp', ('mem', 'ctx')), may hold values from -910 to 910
- window_values: bfloat16 [2, 49152, 32, 128], P('dp', ('mem', 'ctx')), may hold values from -6 to 6
- mem_keys: bfloat16 [144, 32, 64, 128], P('mem'), may hold values from -910 to 910
- mem_values: bfloat16 [144, 32, 64, 128], P('mem'), may hold values from -6 to 6
- gate_logit: float32 [32], replicated, may hold values from -3 to 3
- block_ids: int32 [2, 384, 32], P('dp', ('mem', 'ctx')), may hold values from 0 to 143, as said below
Outputs:
- attended: bfloat16 [2, 49152, 32, 128], P('dp', ('mem', 'ctx'))
Inputs may be any that keep to these rules, and one draw needn't show every extreme that they name: `block_ids`: block b is held by index b // 3 of mem. Among the 32 blocks of one query block, at most 1 are held by one index of mem, and some index of mem holds exactly 1 of them.
All inputs are finite; a program needn't handle non-finite values.
Results may differ from a plain program's by a relative error of at most 0.013.
Values may be sent and summed in bfloat16 or wider, within the bound.
A program may use at most 64 MiB of HBM per device.

v0:
```python
import jax
import jax.numpy as jnp
from jax import lax
from jax.sharding import PartitionSpec as P

W = 128


def shifted(block, axis, distance):
    devices = range(lax.axis_size(axis))
    route = [(i - distance, i) for i in devices if i - distance in devices]
    return lax.ppermute(block, axis, route)


def softmax_rows(scores, allowed):
    masked = jnp.where(allowed, scores, -1e30)
    highest = jnp.max(masked, axis=-1, keepdims=True)
    weights = jnp.where(allowed, jnp.exp(masked - highest), 0.0)
    return (weights / jnp.sum(weights, axis=-1, keepdims=True)).astype(jnp.bfloat16)


def local_attention(query_rows, keys_all, values_all, group_start, softmax_scale):
    row_count = query_rows.shape[0]
    key_count = keys_all.shape[0]
    reach_back = key_count - row_count
    scores = (
        jnp.einsum("qhd,khd->hqk", query_rows, keys_all, preferred_element_type=jnp.float32)
        * softmax_scale
    )
    query_pos = jnp.arange(row_count, dtype=jnp.int32)[:, None]
    key_pos = jnp.arange(key_count, dtype=jnp.int32)[None, :]
    allowed = (
        (key_pos > query_pos)
        & (key_pos <= query_pos + reach_back)
        & (group_start - reach_back + key_pos >= 0)
    )
    weights = softmax_rows(scores, allowed[None])
    return jnp.einsum("hqk,khd->qhd", weights, values_all, preferred_element_type=jnp.float32)


def local(queries, window_keys, window_values, mem_keys, mem_values, gate_logit, block_ids):
    tok_rows = queries.shape[1]
    head_count = queries.shape[2]
    head_size = queries.shape[3]
    softmax_scale = head_size ** (-0.5)
    query_rows = queries[0]
    tail_pair = jnp.stack([window_keys[0, tok_rows - W :], window_values[0, tok_rows - W :]])
    earlier = shifted(tail_pair, ("mem", "ctx"), 1)
    keys_all = jnp.concatenate([earlier[0], window_keys[0]], axis=0)
    values_all = jnp.concatenate([earlier[1], window_values[0]], axis=0)
    group_start = lax.axis_index(("mem", "ctx")) * tok_rows
    local_out = local_attention(query_rows, keys_all, values_all, group_start, softmax_scale)
    owners = lax.axis_size("mem")
    held_blocks = mem_keys.shape[0]
    block_len = mem_keys.shape[2]
    capacity = (head_count + owners - 1) // owners
    wanted = block_ids[0, 0]
    owner_of = wanted // held_blocks
    local_block = wanted % held_blocks
    head_ids = jnp.arange(head_count, dtype=jnp.int32)
    same_before = (owner_of[None, :] == owner_of[:, None]) & (head_ids[None, :] < head_ids[:, None])
    slot_rank = jnp.sum(same_before.astype(jnp.int32), axis=1)
    slot_of = owner_of * capacity + slot_rank
    request = (
        jnp.zeros((owners * capacity,), jnp.int32)
        .at[slot_of]
        .set(local_block * head_count + head_ids)
    )
    request = request.reshape(owners, capacity)
    flat_keys = mem_keys.reshape(held_blocks * head_count, block_len, head_size)
    flat_values = mem_values.reshape(held_blocks * head_count, block_len, head_size)
    slot_head = jnp.zeros((owners * capacity,), jnp.int32).at[slot_of].set(head_ids)
    outgoing = jnp.take(query_rows, slot_head, axis=1).reshape(
        tok_rows, owners, capacity, head_size
    )
    query_part = lax.all_to_all(outgoing, "mem", split_axis=1, concat_axis=1, tiled=True)
    request_part = lax.all_to_all(request[None], "mem", split_axis=1, concat_axis=1, tiled=True)
    block_keys = flat_keys[request_part[0]]
    block_values = flat_values[request_part[0]]
    scores = (
        jnp.einsum("tocd,ockd->octk", query_part, block_keys, preferred_element_type=jnp.float32)
        * softmax_scale
    )
    weights = softmax_rows(scores, True)
    answer = jnp.einsum(
        "octk,ockd->tocd", weights, block_values, preferred_element_type=jnp.float32
    )
    answers = lax.all_to_all(
        answer.astype(jnp.bfloat16), "mem", split_axis=1, concat_axis=1, tiled=True
    )
    memory_out = answers.reshape(tok_rows, owners * capacity, head_size)[:, slot_of]
    gate_mix = jax.nn.sigmoid(gate_logit)[None, :, None]
    mixed = gate_mix * memory_out.astype(jnp.float32) + (1.0 - gate_mix) * local_out
    return mixed.astype(jnp.bfloat16)[None]


def solution(mesh):
    placed = (
        P("dp", ("mem", "ctx"), None, None),
        P("dp", ("mem", "ctx"), None, None),
        P("dp", ("mem", "ctx"), None, None),
        P("mem", None, None, None),
        P("mem", None, None, None),
        P(),
        P("dp", ("mem", "ctx"), None),
    )
    return jax.shard_map(
        local,
        mesh=mesh,
        in_specs=placed,
        out_specs=P("dp", ("mem", "ctx"), None, None),
        check_vma=False,
    )
```

profile of v0, /device:TPU:6, one launch (start us, length us, event | category | flops | bytes accessed | tf_op | source)
XLA Modules:
  0.0 232.3 jit_solution(6424458906559402115)
XLA Ops:
  0.0 0.8 fusion.36
  0.8 0.2 convert_reduce_fusion
  1.0 0.7 fusion.37
  1.6 0.7 scatter_custom_fusion
  2.3 0.7 copy.46
  3.0 18.5 %all-to-all-start = ((s32[1,48,1]{2,0,1:T(1,128)}), s32[1,48,1]{2,0,1:T(1,128)S(1)}, u32[]{:S(2)}, u32[]{:S(2)}) async-start(s32[1,48,1]{2,0,1:T(1,128)} %copy.46), calls=%async_computation | async-start | bytes 49152 | tf_op jit(solution)/shard_map/all_to_all | solution.py:77
  21.6 0.7 scatter_custom_fusion.1
  22.3 1.6 copy.65
  24.0 2.0 gather_fusion.1
  25.9 2.8 %fusion.16 = bf16[128,48,1,128]{3,0,2,1:T(8,128)(2,1)} fusion(bf16[48,128,128]{2,1,0:T(8,128)(2,1)} %gather_fusion.1, pred[48]{0:T(512)(128)(4,1)S(1)} %compare_and_fusion), kind=kLoop, calls=%fused_computation.29 | loop fusion | flops 786432 | bytes 3145776 | tf_op jit(solution)/shard_map/jit(_take)/select_n | solution.py:73
  28.7 3.2 %all-to-all-done = s32[1,48,1]{2,0,1:T(1,128)S(1)} async-done(((s32[1,48,1]{2,0,1:T(1,128)}), s32[1,48,1]{2,0,1:T(1,128)S(1)}, u32[]{:S(2)}, u32[]{:S(2)}) %all-to-all-start) | async-done | bytes 224 | tf_op jit(solution)/shard_map/all_to_all | solution.py:77
  31.9 9.3 %all-to-all-start.1 = ((bf16[128,48,1,128]{3,0,2,1:T(8,128)(2,1)}), bf16[128,48,1,128]{3,0,2,1:T(8,128)(2,1)S(1)}, u32[]{:S(2)}, u32[]{:S(2)}) async-start(bf16[128,48,1,128]{3,0,2,1:T(8,128)(2,1)} %fusion.16), calls=%async_computation.1 | async-start | bytes 3145728 | tf_op jit(solution)/shard_map/all_to_all | solution.py:76
  41.1 0.9 reduce.4
  42.1 1.6 gather_fusion
  43.7 3.0 %gather_fusion.2 = bf16[48,64,128]{2,1,0:T(8,128)(2,1)} fusion(bf16[96,64,128]{2,1,0:T(8,128)(2,1)} %bitcast.94, s32[1024]{0:T(1024)S(1)} %pad_clamp_fusion.2), kind=kCustom, calls=%fused_computation.2 | custom fusion | bytes 1573056 | tf_op jit(solution)/shard_map/gather | solution.py:78
  46.6 52.4 %all-to-all-done.1 = bf16[128,48,1,128]{3,0,2,1:T(8,128)(2,1)S(1)} async-done(((bf16[128,48,1,128]{3,0,2,1:T(8,128)(2,1)}), bf16[128,48,1,128]{3,0,2,1:T(8,128)(2,1)S(1)}, u32[]{:S(2)}, u32[]{:S(2)}) %all-to-all-start.1) | async-done | bytes 1572896 | tf_op jit(solution)/shard_map/all_to_all | solution.py:76
  99.1 2.3 fusion.21
  101.4 1.2 copy-done.4
  102.6 0.3 fusion.49
  102.9 4.2 %fusion.19 = bf16[128,48,1,128]{0,3,2,1:T(8,128)(2,1)} fusion(bf16[48,64,128]{2,1,0:T(8,128)(2,1)} %gather_fusion, f32[48,128]{1,0:T(8,128)S(1)} %fusion.49, f32[48,128,64]{1,2,0:T(8,128)} %copy-done.4), kind=kOutput, calls=%fused_computation.33 | convolution fusion | flops 102635584 | bytes 3956736 | tf_op jit(solution)/shard_map/octk,ockd->tocd/dot_general | solution.py:85
  107.1 6.1 %all-to-all-start.2 = ((bf16[128,48,1,128]{0,3,2,1:T(8,128)(2,1)}), bf16[128,48,1,128]{0,3,2,1:T(8,128)(2,1)}, u32[]{:S(2)}, u32[]{:S(2)}) async-start(bf16[128,48,1,128]{0,3,2,1:T(8,128)(2,1)} %fusion.19), calls=%async_computation.2 | async-start | bytes 3145728 | tf_op jit(solution)/shard_map/all_to_all | solution.py:88
  113.2 1.7 copy.67
  114.9 0.4 copy.66
  115.3 1.7 pad_maximum_fusion
  117.0 3.5 %collective-permute-start = (bf16[2,128,32,128]{3,1,2,0:T(8,128)(2,1)}, bf16[2,128,32,128]{3,1,2,0:T(8,128)(2,1)}, u32[]{:S(2)}, u32[]{:S(2)}) collective-permute-start(bf16[2,128,32,128]{3,1,2,0:T(8,128)(2,1)} %pad_maximum_fusion), channel_id=1, source_target_pairs={{0,2},{2,4},{4,6},{6,8},{8,10},{10,12},{12,14},{14,16},{16,18},{18... | collective-permute-start | bytes 6291464 | tf_op jit(solution)/shard_map/ppermute | solution.py:12
  120.7 94.1 %collective-permute-done = bf16[2,128,32,128]{3,1,2,0:T(8,128)(2,1)} collective-permute-done((bf16[2,128,32,128]{3,1,2,0:T(8,128)(2,1)}, bf16[2,128,32,128]{3,1,2,0:T(8,128)(2,1)}, u32[]{:S(2)}, u32[]{:S(2)}) %collective-permute-start) | collective-permute-done | bytes 2097184 | tf_op jit(solution)/shard_map/ppermute | solution.py:12
  214.8 2.8 %slice_bitcast_fusion.1 = (bf16[128,32,128]{2,0,1:T(8,128)(2,1)}, bf16[128,32,128]{2,0,1:T(8,128)(2,1)S(1)}) fusion(bf16[2,128,32,128]{3,1,2,0:T(8,128)(2,1)} %collective-permute-done), kind=kLoop, calls=%fused_computation.38 | loop fusion | bytes 4194304 | tf_op jit(solution)/shard_map/squeeze | solution.py:50
  217.5 0.8 fusion.7
  218.3 3.2 %fusion.48 = (f32[32,128]{1,0:T(8,128)S(1)}, f32[32,128,256]{1,2,0:T(8,128)}) fusion(f32[32,256,128]{2,1,0:T(8,128)S(1)} %fusion.7, pred[128,256]{0,1:T(8,128)(4,1)S(1)} %fusion.31), kind=kOutput, calls=%fused_computation.82 | output fusion | flops 7340287 | bytes 8437760 | tf_op jit(solution)/shard_map/sub | solution.py:18
  221.6 3.2 %gather_fusion.3 = bf16[32,128,128]{1,2,0:T(8,128)(2,1)} fusion(bf16[128,48,128]{0,2,1:T(8,128)(2,1)} %bitcast.19, s32[1024]{0:T(1024)S(1)} %pad_clamp_fusion), kind=kCustom, calls=%fused_computation.3 | custom fusion | bytes 2097280 | tf_op jit(solution)/shard_map/gather | solution.py:91
  224.7 4.9 %fusion.26 = bf16[1,128,32,128]{1,3,2,0:T(8,128)(2,1)} fusion(f32[32,128,256]{1,2,0:T(8,128)} %get-tuple-element.16, f32[32,128]{1,0:T(8,128)S(1)} %get-tuple-element.15, bf16[128,32,128]{2,0,1:T(8,128)(2,1)S(1)} %bitcast.93, bf16[128,32,128]{2,0,1:T(8,128)(2,1)} %get-tuple-element.7, bf16[32,128,128]{1,2,0:T(8,128)(2,1)} %gather_fusion.3, ...), kind=kOutput, calls=%fused_computation.36 | convolution fusion | flops 277348352 | bytes 8405248 | tf_op jit(solution)/shard_map/hqk,khd->qhd/dot_general | solution.py:38
  229.7 2.6 %copy.56 = bf16[1,128,32,128]{3,2,1,0:T(8,128)(2,1)} copy(bf16[1,128,32,128]{1,3,2,0:T(8,128)(2,1)} %fusion.26) | data formatting | bytes 2097152 | tf_op jit(solution)/shard_map/broadcast_in_dim | solution.py:94
  (25 shorter events, 0.2 us)
Async XLA Ops:
  0.0 42.1 %copy-start = (bf16[3,32,64,128]{3,2,1,0:T(8,128)(2,1)S(1)}, bf16[3,32,64,128]{3,2,1,0:T(8,128)(2,1)}, u32[]{:S(2)}) copy-start(bf16[3,32,64,128]{3,2,1,0:T(8,128)(2,1)} %param.11) | copy-start | bytes 4718596
  3.0 28.8 %all-to-all-start = ((s32[1,48,1]{2,0,1:T(1,128)}), s32[1,48,1]{2,0,1:T(1,128)S(1)}, u32[]{:S(2)}, u32[]{:S(2)}) async-start(s32[1,48,1]{2,0,1:T(1,128)} %copy.46), calls=%async_computation | async-start | bytes 49152 | tf_op jit(solution)/shard_map/all_to_all | solution.py:77
  31.9 67.2 %all-to-all-start.1 = ((bf16[128,48,1,128]{3,0,2,1:T(8,128)(2,1)}), bf16[128,48,1,128]{3,0,2,1:T(8,128)(2,1)S(1)}, u32[]{:S(2)}, u32[]{:S(2)}) async-start(bf16[128,48,1,128]{3,0,2,1:T(8,128)(2,1)} %fusion.16), calls=%async_computation.1 | async-start | bytes 3145728 | tf_op jit(solution)/shard_map/all_to_all | solution.py:76
  101.4 1.2 copy-start.4
  107.1 114.5 %all-to-all-start.2 = ((bf16[128,48,1,128]{0,3,2,1:T(8,128)(2,1)}), bf16[128,48,1,128]{0,3,2,1:T(8,128)(2,1)}, u32[]{:S(2)}, u32[]{:S(2)}) async-start(bf16[128,48,1,128]{0,3,2,1:T(8,128)(2,1)} %fusion.19), calls=%async_computation.2 | async-start | bytes 3145728 | tf_op jit(solution)/shard_map/all_to_all | solution.py:88
  113.1 1.7 copy-start.5
  115.3 1.7 copy-start.2
  115.3 5.3 %copy-start.6 = (f32[32]{0:T(128)S(1)}, f32[32]{0:T(128)}, u32[]{:S(2)}) copy-start(f32[32]{0:T(128)} %param.12) | copy-start | bytes 388
  117.0 97.7 %collective-permute-start = (bf16[2,128,32,128]{3,1,2,0:T(8,128)(2,1)}, bf16[2,128,32,128]{3,1,2,0:T(8,128)(2,1)}, u32[]{:S(2)}, u32[]{:S(2)}) collective-permute-start(bf16[2,128,32,128]{3,1,2,0:T(8,128)(2,1)} %pad_maximum_fusion), channel_id=1, source_target_pairs={{0,2},{2,4},{4,6},{6,8},{8,10},{10,12},{12,14},{14,16},{16,18},{18... | collective-permute-start | bytes 6291464 | tf_op jit(solution)/shard_map/ppermute | solution.py:12
  120.7 96.8 %copy-start.1 = (bf16[1,128,32,128]{3,2,1,0:T(8,128)(2,1)S(1)}, bf16[1,128,32,128]{3,2,1,0:T(8,128)(2,1)}, u32[]{:S(2)}) copy-start(bf16[1,128,32,128]{3,2,1,0:T(8,128)(2,1)} %param.7) | copy-start | bytes 3145732
  221.6 3.2 %copy-start.3 = (bf16[1,128,32,128]{3,1,2,0:T(8,128)(2,1)S(1)}, bf16[1,128,32,128]{3,1,2,0:T(8,128)(2,1)}, u32[]{:S(2)}) copy-start(bf16[1,128,32,128]{3,1,2,0:T(8,128)(2,1)} %copy-done.2) | copy-start | bytes 3145732
where the time goes:
time: 233 us; the launch traced here: 232 us
  waiting for transfers between devices  150 us (64%)
  starting transfers between devices  37.4 us (16%)
  local copies, waits for them, and re-layouts  22 us (9%)
  matrix products  12.2 us (5%)
  other arithmetic  10.8 us (5%)
    ppermute x1, waiting for transfers between devices, shifted(): return lax.ppermute(block, axis, route)  94.1 us
    all_to_all x1, waiting for transfers between devices, local(): lax.all_to_all(outgoing, 'mem', split_axis=1, concat_axis=1, tiled=True)  52.4 us
    all_to_all x1, starting transfers between devices, local(): lax.all_to_all(request[None], 'mem', split_axis=1, concat_axis=1, tiled=T...  18.5 us
    all_to_all x1, starting transfers between devices, local(): lax.all_to_all(outgoing, 'mem', split_axis=1, concat_axis=1, tiled=True)  9.29 us
    all_to_all x1, starting transfers between devices, local(): lax.all_to_all(answer.astype(jnp.bfloat16), 'mem', split_axis=1, concat_a...  6.05 us
    unnamed x17, local copies, waits for them, and re-layouts  4.95 us
    dot_general x1, matrix products, local_attention(): jnp.einsum('hqk,khd->qhd', weights, values_all, preferred_element_type=jn...  4.93 us
  transfers between devices with their start and end apart: 4, of which 3 were waited for; matrix products, arithmetic and copies ran while one was open for 10% of the time, Pallas kernels for 0%

commit v1 on v0

v1 whole, which is shorter than its diff:
```python
import functools

import jax
import jax.numpy as jnp
from jax import lax
from jax.experimental import pallas as pl
from jax.experimental.pallas import tpu as pltpu
from jax.sharding import PartitionSpec as P

MESH = pl.DeviceIdType.MESH
XN = 4
CHUNK = 32
UNROLL = 4
NEG = -1e30


def dot_nt(a, b):
    return lax.dot_general(a, b, (((1,), (1,)), ((), ())), preferred_element_type=jnp.float32)


def dot_nn(a, b):
    return lax.dot_general(a, b, (((1,), (0,)), ((), ())), preferred_element_type=jnp.float32)


def kernel(
    sizes,
    q_hbm, k_hbm, v_hbm, mk_hbm, mv_hbm, gate_sm, ids_sm, req_hbm,
    out_hbm,
    q_v, k_v, v_v, mk_v, mv_v,
    qn_v, ansn_v, ansp_v, stn_v, stp_v,
    wide, q_t, k_t, v_t, qn_t, own_o, own_m,
    tab_v, tab_sm, blk_send, blk_recv,
    load_sem, q_send, q_recv, a_send, a_recv, s_send, s_recv,
    r_send, r_recv, b_send, b_recv, self_sem, tab_sem, out_sem,
):
    xn, zn, cn, held = sizes
    mem_n = xn * zn
    tok, heads, width = q_v.shape
    blk = mk_v.shape[1]
    scale = width ** (-0.5)
    pieces = tok // CHUNK
    mem, ctx, dp = lax.axis_index("mem"), lax.axis_index("ctx"), lax.axis_index("dp")
    mx, mz = mem // zn, mem % zn
    group = mem * cn + ctx
    total = mem_n * cn
    before = (group + total - 1) % total
    after = (group + 1) % total
    prev = (before // cn, before % cn, dp)
    nxt = (after // cn, after % cn, dp)

    def owner_at(k):
        return ((mx + k // zn) % xn) * zn + (mz + k % zn) % zn

    def asker_at(k):
        return ((mx + xn - k // zn) % xn) * zn + (mz + zn - k % zn) % zn

    loads = [
        pltpu.make_async_copy(src, dst, load_sem.at[i])
        for i, (src, dst) in enumerate(
            ((mk_hbm, mk_v), (mv_hbm, mv_v), (k_hbm, k_v), (v_hbm, v_v), (q_hbm, q_v))
        )
    ]
    for load in loads:
        load.start()
    own_row = pltpu.make_async_copy(req_hbm.at[mem], tab_v.at[0], self_sem)
    own_row.start()

    barrier = pltpu.get_barrier_semaphore()
    pl.semaphore_signal(barrier, inc=1, device_id=prev, device_id_type=MESH)
    pl.semaphore_signal(barrier, inc=1, device_id=nxt, device_id_type=MESH)

    def greet(k, _):
        pl.semaphore_signal(barrier, inc=1, device_id=(owner_at(k), ctx, dp), device_id_type=MESH)
        return 0

    lax.fori_loop(1, mem_n, greet, 0)
    pl.semaphore_wait(barrier, mem_n + 1)

    def ask(k, _):
        owner = owner_at(k)
        pltpu.make_async_remote_copy(
            req_hbm.at[owner], tab_v.at[k], r_send, r_recv, (owner, ctx, dp), MESH
        ).start()
        return 0

    lax.fori_loop(1, mem_n, ask, 0)

    def q_piece(c):
        rows = pl.ds(c * CHUNK, CHUNK)
        return pltpu.make_async_remote_copy(
            q_hbm.at[rows], qn_v.at[rows], q_send.at[c], q_recv.at[c], prev, MESH
        )

    for c in range(pieces):
        q_piece(c).start()

    others = pl.ds(1, mem_n - 1)
    ask_all = pltpu.make_async_remote_copy(
        tab_v.at[others], tab_v.at[others], r_send, r_recv, prev, MESH
    )
    loads[0].wait()
    loads[1].wait()
    own_row.wait()
    ask_all.wait_recv()
    to_scalar = pltpu.make_async_copy(tab_v, tab_sm, tab_sem)
    to_scalar.start()
    to_scalar.wait()

    blk_recv[0, pl.ds(0, blk)] = mk_v[tab_sm[0, 0, 0]]
    blk_recv[0, pl.ds(blk, blk)] = mv_v[tab_sm[0, 0, 0]]

    def serve(k, _):
        which = tab_sm[k, 0, 0]
        blk_send[k, pl.ds(0, blk)] = mk_v[which]
        blk_send[k, pl.ds(blk, blk)] = mv_v[which]
        pltpu.make_async_remote_copy(
            blk_send.at[k], blk_recv.at[k], b_send, b_recv, (asker_at(k), ctx, dp), MESH
        ).start()
        return 0

    lax.fori_loop(1, mem_n, serve, 0)

    def widen(src, first, count):
        step = min(count, 16)

        def one(i, _):
            rows = src[pl.ds(first + i * step, step)].astype(jnp.float32)
            wide[pl.ds(i * step * heads, step * heads)] = rows.reshape(step * heads, width)
            return 0

        lax.fori_loop(0, count // step, one, 0)

    def by_head(dst, first, count):
        def some(i, _):
            for u in range(UNROLL):
                h = i * UNROLL + u
                rows = wide[pl.ds(h, count, stride=heads), :]
                dst[h, pl.ds(first, count), pl.ds(0, width)] = rows.astype(jnp.bfloat16)
            return 0

        lax.fori_loop(0, heads // UNROLL, some, 0)

    for i, (src, dst) in ((2, (k_v, k_t)), (3, (v_v, v_t)), (4, (q_v, q_t))):
        loads[i].wait()
        widen(src, 0, tok)
        by_head(dst, 0, tok)

    def ones_half(h, _):
        v_t[h, :, pl.ds(width, width)] = jnp.ones((tok, width), jnp.bfloat16)
        return 0

    lax.fori_loop(0, heads, ones_half, 0)

    q_pos = lax.broadcasted_iota(jnp.int32, (tok, tok), 0)
    k_pos = lax.broadcasted_iota(jnp.int32, (tok, tok), 1)
    causal = k_pos <= q_pos

    def own(i, _):
        for u in range(UNROLL):
            h = i * UNROLL + u
            scores = jnp.where(causal, dot_nt(q_t[h], k_t[h]) * scale, NEG)
            top = jnp.max(scores, axis=-1, keepdims=True)
            weights = jnp.exp(scores - top).astype(jnp.bfloat16)
            own_o[h] = dot_nn(weights, v_t[h])
            own_m[h] = jnp.broadcast_to(top, (tok, width))
        return 0

    lax.fori_loop(0, heads // UNROLL, own, 0)

    lane = lax.broadcasted_iota(jnp.int32, (CHUNK, width), 1)

    def a_piece(c):
        rows = pl.ds(c * CHUNK, CHUNK)
        return pltpu.make_async_remote_copy(
            ansn_v.at[rows], ansp_v.at[rows], a_send.at[c], a_recv.at[c], nxt, MESH
        )

    def s_piece(c):
        rows = pl.ds(c * CHUNK, CHUNK)
        return pltpu.make_async_remote_copy(
            stn_v.at[rows], stp_v.at[rows], s_send.at[c], s_recv.at[c], nxt, MESH
        )

    for c in range(pieces):
        q_piece(c).wait_recv()
        widen(qn_v, c * CHUNK, CHUNK)
        by_head(qn_t, 0, CHUNK)
        past = k_pos[:CHUNK] > q_pos[:CHUNK] + c * CHUNK

        def partial(i, stats, past=past):
            for u in range(UNROLL):
                h = i * UNROLL + u
                scores = jnp.where(past, dot_nt(qn_t[h], k_t[h]) * scale, NEG)
                top = jnp.max(scores, axis=-1, keepdims=True)
                weights = jnp.where(past, jnp.exp(scores - top), 0.0).astype(jnp.bfloat16)
                summed = dot_nn(weights, v_t[h])
                wide[pl.ds(h, CHUNK, stride=heads), :] = summed[:, :width]
                stats = jnp.where(lane == h, top, stats)
                stats = jnp.where(lane == h + heads, summed[:, width:], stats)
            return stats

        stats = lax.fori_loop(
            0, heads // UNROLL, partial, jnp.zeros((CHUNK, width), jnp.float32)
        )
        stn_v[pl.ds(c * CHUNK, CHUNK)] = stats

        def narrow(i, _, c=c):
            step = 16
            rows = wide[pl.ds(i * step * heads, step * heads)].reshape(step, heads, width)
            ansn_v[pl.ds(c * CHUNK + i * step, step)] = rows.astype(jnp.bfloat16)
            return 0

        lax.fori_loop(0, CHUNK // 16, narrow, 0)
        a_piece(c).start()
        s_piece(c).start()

    lane_all = lax.broadcasted_iota(jnp.int32, (tok, width), 1)
    first_block = group == 0

    for c in range(pieces):
        a_piece(c).wait_recv()
        s_piece(c).wait_recv()
    widen(ansp_v, 0, tok)

    def gate_of(h):
        return 1.0 / (1.0 + jnp.exp(jnp.full((8, width), -gate_sm[h], jnp.float32)))[:1]

    def join(i, _):
        stats = stp_v[...]
        for u in range(UNROLL):
            h = i * UNROLL + u
            top_p = jnp.sum(jnp.where(lane_all == h, stats, 0.0), axis=-1, keepdims=True)
            sum_p = jnp.sum(jnp.where(lane_all == h + heads, stats, 0.0), axis=-1, keepdims=True)
            top_p = jnp.where(first_block, NEG, top_p)
            top_o = own_m[h]
            top = jnp.maximum(top_p, top_o)
            part_p = jnp.exp(top_p - top)
            part_o = jnp.exp(top_o - top)
            mine = own_o[h]
            theirs = wide[pl.ds(h, tok, stride=heads), :]
            above = part_p * theirs + part_o * mine[:, :width]
            below = part_p * sum_p + part_o * mine[:, width:]
            own_m[h] = (1.0 - gate_of(h)) * (above / below)
        return 0

    lax.fori_loop(0, heads // UNROLL, join, 0)

    block_all = pltpu.make_async_remote_copy(
        blk_send.at[others], blk_recv.at[others], b_send, b_recv, prev, MESH
    )
    block_all.wait_recv()

    def recall(i, _):
        for u in range(UNROLL):
            h = i * UNROLL + u
            owner = lax.div(ids_sm[h], held)
            dx = lax.rem(lax.div(owner, zn) - mx + xn, xn)
            dz = lax.rem(lax.rem(owner, zn) - mz + zn, zn)
            block = blk_recv[dx * zn + dz]
            scores = dot_nt(q_t[h], block[:blk]) * scale
            top = jnp.max(scores, axis=-1, keepdims=True)
            weights = jnp.exp(scores - top)
            below = jnp.sum(weights, axis=-1, keepdims=True)
            above = dot_nn(weights.astype(jnp.bfloat16), block[blk:])
            mixed = gate_of(h) * (above / below) + own_m[h]
            wide[pl.ds(h, tok, stride=heads), :] = mixed
        return 0

    lax.fori_loop(0, heads // UNROLL, recall, 0)

    def finish(i, _):
        step = 16
        rows = wide[pl.ds(i * step * heads, step * heads)].reshape(step, heads, width)
        q_v[pl.ds(i * step, step)] = rows.astype(jnp.bfloat16)
        return 0

    lax.fori_loop(0, tok // 16, finish, 0)
    result = pltpu.make_async_copy(q_v, out_hbm, out_sem)
    result.start()
    ask_all.wait_send()
    block_all.wait_send()
    for c in range(pieces):
        q_piece(c).wait_send()
        a_piece(c).wait_send()
        s_piece(c).wait_send()
    result.wait()


def local(queries, window_keys, window_values, mem_keys, mem_values, gate_logit, block_ids):
    _, tok, heads, width = queries.shape
    held, _, blk, _ = mem_keys.shape
    mem_n, cn = lax.axis_size("mem"), lax.axis_size("ctx")
    zn = mem_n // XN
    pieces = tok // CHUNK
    wanted = block_ids[0, 0]
    head_ids = jnp.arange(heads, dtype=jnp.int32)
    entry = (wanted % held) * heads + head_ids
    asked = jnp.where(
        (wanted // held)[None, :] == jnp.arange(mem_n, dtype=jnp.int32)[:, None], entry[None, :], 0
    )
    request = jnp.broadcast_to(jnp.sum(asked, axis=1)[:, None, None], (mem_n, 1, 128))
    anywhere = pl.BlockSpec(memory_space=pl.ANY)
    scalars = pl.BlockSpec(memory_space=pltpu.SMEM)
    bf, f32 = jnp.bfloat16, jnp.float32
    dma = pltpu.SemaphoreType.DMA
    native = pltpu.VMEM((tok, heads, width), bf)
    out = pl.pallas_call(
        functools.partial(kernel, (XN, zn, cn, held)),
        out_shape=jax.ShapeDtypeStruct((tok, heads, width), bf),
        in_specs=[anywhere] * 5 + [scalars, scalars, anywhere],
        out_specs=anywhere,
        scratch_shapes=[
            native, native, native,
            pltpu.VMEM((held * heads, blk, width), bf),
            pltpu.VMEM((held * heads, blk, width), bf),
            native, native, native,
            pltpu.VMEM((tok, width), f32),
            pltpu.VMEM((tok, width), f32),
            pltpu.VMEM((tok * heads, width), f32),
            pltpu.VMEM((heads, tok, width), bf),
            pltpu.VMEM((heads, tok, width), bf),
            pltpu.VMEM((heads, tok, 2 * width), bf),
            pltpu.VMEM((heads, CHUNK, width), bf),
            pltpu.VMEM((heads, tok, 2 * width), f32),
            pltpu.VMEM((heads, tok, width), f32),
            pltpu.VMEM((mem_n, 1, 128), jnp.int32),
            pltpu.SMEM((mem_n, 1, 128), jnp.int32),
            pltpu.VMEM((mem_n, 2 * blk, width), bf),
            pltpu.VMEM((mem_n, 2 * blk, width), bf),
            dma((5,)), dma((pieces,)), dma((pieces,)), dma((pieces,)), dma((pieces,)),
            dma((pieces,)), dma((pieces,)),
            dma, dma, dma, dma, dma, dma, dma,
        ],
        compiler_params=pltpu.CompilerParams(
            collective_id=0, has_side_effects=True, vmem_limit_bytes=56 * 1024 * 1024
        ),
    )(
        queries[0], window_keys[0], window_values[0],
        mem_keys.reshape(held * heads, blk, width), mem_values.reshape(held * heads, blk, width),
        gate_logit, wanted, request,
    )
    return out[None]


def solution(mesh):
    placed = (
        P("dp", ("mem", "ctx"), None, None),
        P("dp", ("mem", "ctx"), None, None),
        P("dp", ("mem", "ctx"), None, None),
        P("mem", None, None, None),
        P("mem", None, None, None),
        P(),
        P("dp", ("mem", "ctx"), None),
    )
    return jax.shard_map(
        local,
        mesh=mesh,
        in_specs=placed,
        out_specs=P("dp", ("mem", "ctx"), None, None),
        check_vma=False,
    )
```

time: 233 us -> 127 us (0.55)
  the two profiles are of different devices: /device:TPU:6 before, /device:TPU:1 now
where the time goes in v1:
time: 127 us
  Pallas kernels  123 us (97%)
  local copies, waits for them, and re-layouts  2.99 us (2%)
    pallas_call x1, Pallas kernels, local(): pl.pallas_call(functools.partial(kernel, (XN, zn, cn, held)), out_shape=j...  123 us

profile of v1, /device:TPU:1, one launch (start us, length us, event | category | flops | bytes accessed | tf_op | source)
XLA Modules:
  0.0 126.5 jit_solution(6727976070182088690)
XLA Ops:
  0.0 0.7 and_select_fusion.1
  0.7 0.1 select_reduce_fusion
  0.8 0.7 broadcast_in_dim.26.req_hbm
  1.5 122.8 %shard_map.73 = bf16[128,32,128]{2,1,0:T(8,128)(2,1)} custom-call(bf16[128,32,128]{2,1,0:T(8,128)(2,1)} %bitcast.12, bf16[128,32,128]{2,1,0:T(8,128)(2,1)} %bitcast.13, bf16[128,32,128]{2,1,0:T(8,128)(2,1)} %bitcast.14, bf16[96,64,128]{2,1,0:T(8,128)(2,1)} %bitcast.10, bf16[96,64,128]{2,1,0:T(8,128)(2,1)} %bitcast.11, f32[32]{0:T(128)} %gate_sm.1, ...), custom_call_target="tpu_custom_call" | custom-call | tf_op jit(solution)/shard_map/pallas_call | solution.py:307
  124.3 2.3 %copy.9 = bf16[1,128,32,128]{3,2,1,0:T(8,128)(2,1)} copy(bf16[1,128,32,128]{3,2,1,0:T(8,128)(2,1)} %bitcast.9) | data formatting | bytes 2097152

commit v2 on v1

v2 whole, which is shorter than its diff:
```python
import functools

import jax
import jax.numpy as jnp
from jax import lax
from jax.experimental import pallas as pl
from jax.experimental.pallas import tpu as pltpu
from jax.sharding import PartitionSpec as P

MESH = pl.DeviceIdType.MESH
XN = 4
CHUNK = 32
UNROLL = 4
NEG = -1e30
AHEAD = 4
DOWN, UP = 17, 28
BOTH, NOT_FIRST, NOT_LAST = range(3)
PLAN = (
    ((20, 4, NOT_FIRST), (28, 4, NOT_LAST)),
    ((17, 3, NOT_FIRST), (32, 3, NOT_LAST), (16, 1, BOTH), (35, 1, BOTH)),
    ((12, 4, BOTH), (36, 4, BOTH)),
    ((8, 4, BOTH), (40, 4, BOTH)),
    ((24, 3, BOTH), (1, 3, BOTH), (27, 1, BOTH)),
    ((4, 4, BOTH), (44, 4, BOTH)),
)
EXTRA = 1


def dot_nt(a, b):
    return lax.dot_general(a, b, (((1,), (1,)), ((), ())), preferred_element_type=jnp.float32)


def dot_nn(a, b):
    return lax.dot_general(a, b, (((1,), (0,)), ((), ())), preferred_element_type=jnp.float32)


def kernel(
    sizes,
    q_hbm, k_hbm, v_hbm, mk_hbm, mv_hbm, gate_sm, ids_sm, req_hbm,
    out_hbm,
    q_v, k_v, v_v, mk_v, mv_v,
    qn_v, ansn_v, ansp_v, stn_v, stp_v,
    q_t, k_t, v_t, qn_t, an_t, ap_t, own_o, own_m, mem_w,
    tab_v, tab_sm, mk_send, mk_recv, mv_send, mv_recv,
    load_sem, q_send, q_recv, a_send, a_recv, s_send, s_recv, far_send, far_recv,
    r_send, r_recv, b_send, b_recv, self_sem, tab_sem, out_sem,
):
    xn, zn, cn, held = sizes
    mem_n = xn * zn
    tok, heads, width = q_v.shape
    blk = mk_v.shape[1]
    scale = width ** (-0.5)
    sub = tok // cn
    mem, ctx, dp = lax.axis_index("mem"), lax.axis_index("ctx"), lax.axis_index("dp")
    mx, mz = mem // zn, mem % zn
    group = mem * cn + ctx
    total = mem_n * cn
    before = (group + total - 1) % total
    after = (group + 1) % total
    prev = (before // cn, before % cn, dp)
    nxt = (after // cn, after % cn, dp)
    first_ctx, last_ctx = ctx == 0, ctx == cn - 1
    not_first, not_last = ctx > 0, ctx < cn - 1
    down, up = DOWN + ctx - 1, UP + ctx

    def owner_at(k):
        return ((mx + k % xn) % xn) * zn + (mz + k // xn) % zn

    def asker_at(k):
        return ((mx + xn - k % xn) % xn) * zn + (mz + zn - k // xn) % zn

    loads = [
        pltpu.make_async_copy(src, dst, load_sem.at[i])
        for i, (src, dst) in enumerate(
            ((k_hbm, k_v), (mk_hbm, mk_v), (mv_hbm, mv_v), (v_hbm, v_v), (q_hbm, q_v))
        )
    ]
    for load in loads:
        load.start()
    own_row = pltpu.make_async_copy(req_hbm.at[mem], tab_v.at[0], self_sem)
    own_row.start()

    barrier = pltpu.get_barrier_semaphore()

    def greet(k, _):
        pl.semaphore_signal(barrier, inc=1, device_id=(owner_at(k), ctx, dp), device_id_type=MESH)
        return 0

    lax.fori_loop(1, mem_n, greet, 0)

    def greet_at(there):
        pl.semaphore_signal(barrier, inc=1, device_id=there, device_id_type=MESH)

    greet_at(prev)
    greet_at(nxt)

    @pl.when(first_ctx)
    def _():
        for j in range(1, cn):
            greet_at((owner_at(DOWN + j - 1), j, dp))

    @pl.when(last_ctx)
    def _():
        for j in range(cn - 1):
            greet_at((owner_at(UP + j), j, dp))

    pl.when(not_first)(lambda: greet_at((asker_at(down), 0, dp)))
    pl.when(not_last)(lambda: greet_at((asker_at(up), cn - 1, dp)))
    pl.when(first_ctx | last_ctx)(lambda: pl.semaphore_wait(barrier, mem_n + 1 + cn))
    pl.when(not_first & not_last)(lambda: pl.semaphore_wait(barrier, mem_n + 1 + 2))

    def ask(k, _):
        owner = owner_at(k)
        pltpu.make_async_remote_copy(
            req_hbm.at[owner], tab_v.at[k], r_send, r_recv, (owner, ctx, dp), MESH
        ).start()
        return 0

    lax.fori_loop(1, mem_n, ask, 0)

    def ask_aside(k, j, i):
        owner = owner_at(k)
        return pltpu.make_async_remote_copy(
            req_hbm.at[owner], tab_v.at[mem_n + i], far_send.at[j], far_recv.at[i], (owner, j, dp), MESH
        )

    @pl.when(first_ctx)
    def _():
        for j in range(1, cn):
            ask_aside(DOWN + j - 1, j, 0).start()

    @pl.when(last_ctx)
    def _():
        for j in range(cn - 1):
            ask_aside(UP + j, j, 1).start()

    def rows_of(c):
        return pl.ds(c * sub, sub)

    def q_direct(c):
        return pltpu.make_async_remote_copy(
            q_hbm.at[rows_of(c)], qn_v.at[rows_of(c)], q_send.at[c], q_recv.at[c], prev, MESH
        )

    def q_start(c):
        q_direct(c).start()

    for c in range(min(4, cn)):
        q_start(c)

    def by_head(dst, src, first, count):
        def one(i, _):
            rows = src[pl.ds(first + i * 16, 16)]
            dst[:, pl.ds(i * 16, 16), pl.ds(0, width)] = jnp.swapaxes(rows, 0, 1)
            return 0

        lax.fori_loop(0, count // 16, one, 0)

    def by_position(dst, src, first, count):
        def one(i, _):
            dst[pl.ds(first + i * 16, 16)] = jnp.swapaxes(src[:, pl.ds(i * 16, 16), :], 0, 1)
            return 0

        lax.fori_loop(0, count // 16, one, 0)

    def some_heads(count, body, init=0, first=0, last=heads):
        def one(i, carry):
            return body([i * count + u for u in range(count)], carry)

        return lax.fori_loop(first // count, last // count, one, init)

    loads[0].wait()
    by_head(k_t, k_v, 0, tok)

    others = pl.ds(1, mem_n - 1)
    ask_all = pltpu.make_async_remote_copy(
        tab_v.at[others], tab_v.at[others], r_send, r_recv, prev, MESH
    )
    loads[1].wait()
    own_row.wait()
    ask_all.wait_recv()
    pl.when(not_first)(lambda: ask_aside(0, 0, 0).wait_recv())
    pl.when(not_last)(lambda: ask_aside(0, 0, 1).wait_recv())
    to_scalar = pltpu.make_async_copy(tab_v, tab_sm, tab_sem)
    to_scalar.start()
    to_scalar.wait()

    batches = len(PLAN)
    who = {BOTH: None, NOT_FIRST: not_first, NOT_LAST: not_last}
    extras = {(EXTRA, NOT_FIRST): (mem_n, down, 0), (EXTRA, NOT_LAST): (mem_n + 1, up, cn - 1)}

    def guarded(part, act):
        if who[part] is None:
            act()
        else:
            pl.when(who[part])(act)

    def batch_done(i):
        send = (mk_send, mv_send)[i // batches]
        for r, (first, count, part) in enumerate(PLAN[i % batches]):
            sent = pl.ds(0, count + int((i % batches, part) in extras))
            copy = pltpu.make_async_remote_copy(
                send.at[sent], send.at[sent], b_send.at[i, r], b_recv.at[0], prev, MESH
            )
            guarded(part, copy.wait_send)

    def serve(i):
        send, recv = ((mk_send, mk_recv), (mv_send, mv_recv))[i // batches]
        held_v = (mk_v, mv_v)[i // batches]
        if i >= AHEAD:
            batch_done(i - AHEAD)
        if i % batches == 0:
            recv[0] = held_v[tab_sm[0, 0, 0]]

        def push(k, to, r, there):
            send[k] = held_v[tab_sm[k, 0, 0]]
            pltpu.make_async_remote_copy(
                send.at[k], recv.at[to], b_send.at[i, r], b_recv.at[i // batches], there, MESH
            ).start()

        ranges = PLAN[i % batches]
        for r, (first, count, part) in enumerate(ranges):
            if (i % batches, part) in extras:
                k, to, there = extras[i % batches, part]
                guarded(part, lambda k=k, to=to, r=r, y=there: push(k, to, r, (asker_at(to), y, dp)))

        def some(t, _):
            for r, (first, count, part) in enumerate(ranges):
                if count > 1:
                    k = first + t
                    guarded(part, lambda k=k, r=r: push(k, k, r, (asker_at(k), ctx, dp)))
            return 0

        lax.fori_loop(0, min([count for _, count, _ in ranges if count > 1] or [0]), some, 0)
        for r, (first, count, part) in enumerate(ranges):
            if count == 1:
                guarded(part, lambda k=first, r=r: push(k, k, r, (asker_at(k), ctx, dp)))

    steps = iter(range(2 * batches))

    def pump():
        for i in steps:
            serve(i)
            return

    loads[2].wait()
    pump()
    pump()
    for c in range(4, cn):
        q_start(c)
    pump()

    for i, (src, dst) in ((3, (v_v, v_t)), (4, (q_v, q_t))):
        loads[i].wait()
        by_head(dst, src, 0, tok)
    pump()

    def ones_half(h, _):
        v_t[h, :, pl.ds(width, width)] = jnp.ones((tok, width), jnp.bfloat16)
        return 0

    lax.fori_loop(0, heads, ones_half, 0)

    q_pos = lax.broadcasted_iota(jnp.int32, (tok, tok), 0)
    k_pos = lax.broadcasted_iota(jnp.int32, (tok, tok), 1)

    lane = lax.broadcasted_iota(jnp.int32, (CHUNK, width), 1)

    def a_direct(c):
        return pltpu.make_async_remote_copy(
            ansn_v.at[rows_of(c)], ansp_v.at[rows_of(c)], a_send.at[c], a_recv.at[c], nxt, MESH
        )

    def s_piece(c):
        rows = pl.ds(c * CHUNK, CHUNK)
        return pltpu.make_async_remote_copy(
            stn_v.at[rows], stp_v.at[rows], s_send.at[c], s_recv.at[c], nxt, MESH
        )

    per = CHUNK // sub

    def answer(c):
        for j in range(c * per, (c + 1) * per):
            q_direct(j).wait_recv()
        by_head(qn_t, qn_v, c * CHUNK, CHUNK)
        past = k_pos[:CHUNK] > q_pos[:CHUNK] + c * CHUNK

        def partial(hs, stats):
            scores = [dot_nt(qn_t[h], k_t[h]) for h in hs]
            scores = [jnp.where(past, x * scale, NEG) for x in scores]
            tops = [jnp.max(x, axis=-1, keepdims=True) for x in scores]
            weights = [jnp.where(past, jnp.exp(x - t), 0.0) for x, t in zip(scores, tops)]
            summed = [dot_nn(w.astype(jnp.bfloat16), v_t[h]) for w, h in zip(weights, hs)]
            for h, x, t in zip(hs, summed, tops):
                an_t[h] = x[:, :width].astype(jnp.bfloat16)
                stats = jnp.where(lane == h, t, stats)
                stats = jnp.where(lane == h + heads, x[:, width:], stats)
            return stats

        stn_v[pl.ds(c * CHUNK, CHUNK)] = some_heads(
            min(8, heads), partial, jnp.zeros((CHUNK, width), jnp.float32)
        )
        by_position(ansn_v, an_t, c * CHUNK, CHUNK)
        for j in range(c * per, (c + 1) * per):
            a_direct(j).start()
        s_piece(c).start()

    causal = k_pos <= q_pos

    def own(hs, _):
        scores = [dot_nt(q_t[h], k_t[h]) for h in hs]
        scores = [jnp.where(causal, x * scale, NEG) for x in scores]
        tops = [jnp.max(x, axis=-1, keepdims=True) for x in scores]
        weights = [jnp.exp(x - t).astype(jnp.bfloat16) for x, t in zip(scores, tops)]
        summed = [dot_nn(w, v_t[h]) for w, h in zip(weights, hs)]
        for h, x, t in zip(hs, summed, tops):
            own_o[h] = x
            own_m[h] = jnp.broadcast_to(t, (tok, width))
        return 0

    pieces = tok // CHUNK
    for c in range(pieces // 2):
        answer(c)
        pump()
    some_heads(UNROLL, own)
    pump()
    for c in range(pieces // 2, pieces):
        answer(c)
        pump()
    for _ in range(2 * batches):
        pump()

    def gate_of(h):
        return 1.0 / (1.0 + jnp.exp(jnp.full((8, width), -gate_sm[h], jnp.float32)))[:1]

    def slot_of(h):
        owner = lax.div(ids_sm[h], held)
        dx = lax.rem(lax.div(owner, zn) - mx + xn, xn)
        dz = lax.rem(lax.rem(owner, zn) - mz + zn, zn)
        return dz * xn + dx

    def fetched(send, recv, i):
        return pltpu.make_async_remote_copy(
            send.at[others], recv.at[others], b_send.at[0], b_recv.at[i], prev, MESH
        )

    fetched(mk_send, mk_recv, 0).wait_recv()

    def weigh(hs, _):
        scores = [dot_nt(q_t[h], mk_recv[slot_of(h)]) * scale for h in hs]
        tops = [jnp.max(x, axis=-1, keepdims=True) for x in scores]
        weights = [jnp.exp(x - t) for x, t in zip(scores, tops)]
        sums = [jnp.sum(w, axis=-1, keepdims=True) for w in weights]
        for h, w, below in zip(hs, weights, sums):
            mem_w[h] = (w * (gate_of(h)[:, :blk] / below)).astype(jnp.bfloat16)
        return 0

    some_heads(UNROLL, weigh)

    lane_all = lax.broadcasted_iota(jnp.int32, (tok, width), 1)
    first_block = group == 0
    for c in range(cn):
        a_direct(c).wait_recv()
    for c in range(pieces):
        s_piece(c).wait_recv()
    by_head(ap_t, ansp_v, 0, tok)

    def join(hs, _):
        stats = stp_v[...]
        tops_p = [jnp.where(lane_all == h, stats, 0.0) for h in hs]
        sums_p = [jnp.where(lane_all == h + heads, stats, 0.0) for h in hs]
        tops_p = [jnp.sum(x, axis=-1, keepdims=True) for x in tops_p]
        sums_p = [jnp.sum(x, axis=-1, keepdims=True) for x in sums_p]
        for h, top_p, sum_p in zip(hs, tops_p, sums_p):
            top_p = jnp.where(first_block, NEG, top_p)
            top_o = own_m[h]
            top = jnp.maximum(top_p, top_o)
            part_p = jnp.exp(top_p - top)
            part_o = jnp.exp(top_o - top)
            mine = own_o[h]
            above = part_p * ap_t[h].astype(jnp.float32) + part_o * mine[:, :width]
            below = part_p * sum_p + part_o * mine[:, width:]
            own_m[h] = (1.0 - gate_of(h)) * (above / below)
        return 0

    some_heads(UNROLL, join)

    fetched(mv_send, mv_recv, 1).wait_recv()

    def recall(hs, _):
        found = [dot_nn(mem_w[h], mv_recv[slot_of(h)]) for h in hs]
        for h, x in zip(hs, found):
            ap_t[h] = (x + own_m[h]).astype(jnp.bfloat16)
        return 0

    some_heads(min(8, heads), recall)
    by_position(q_v, ap_t, 0, tok)
    result = pltpu.make_async_copy(q_v, out_hbm, out_sem)
    result.start()
    ask_all.wait_send()
    for i in range(max(0, 2 * batches - AHEAD), 2 * batches):
        batch_done(i)
    for c in range(cn):
        q_direct(c).wait_send()
        a_direct(c).wait_send()
    for c in range(pieces):
        s_piece(c).wait_send()

    @pl.when(first_ctx)
    def _():
        for j in range(1, cn):
            ask_aside(DOWN + j - 1, j, 0).wait_send()

    @pl.when(last_ctx)
    def _():
        for j in range(cn - 1):
            ask_aside(UP + j, j, 1).wait_send()

    result.wait()


def local(queries, window_keys, window_values, mem_keys, mem_values, gate_logit, block_ids):
    _, tok, heads, width = queries.shape
    held, _, blk, _ = mem_keys.shape
    mem_n, cn = lax.axis_size("mem"), lax.axis_size("ctx")
    zn = mem_n // XN
    pieces = tok // CHUNK
    wanted = block_ids[0, 0]
    head_ids = jnp.arange(heads, dtype=jnp.int32)
    entry = (wanted % held) * heads + head_ids
    asked = jnp.where(
        (wanted // held)[None, :] == jnp.arange(mem_n, dtype=jnp.int32)[:, None], entry[None, :], 0
    )
    request = jnp.broadcast_to(jnp.sum(asked, axis=1)[:, None, None], (mem_n, 1, 128))
    anywhere = pl.BlockSpec(memory_space=pl.ANY)
    scalars = pl.BlockSpec(memory_space=pltpu.SMEM)
    bf, f32 = jnp.bfloat16, jnp.float32
    dma = pltpu.SemaphoreType.DMA
    native = pltpu.VMEM((tok, heads, width), bf)
    slots = pltpu.VMEM((mem_n + 2, blk, width), bf)
    out = pl.pallas_call(
        functools.partial(kernel, (XN, zn, cn, held)),
        out_shape=jax.ShapeDtypeStruct((tok, heads, width), bf),
        in_specs=[anywhere] * 5 + [scalars, scalars, anywhere],
        out_specs=anywhere,
        scratch_shapes=[
            native, native, native,
            pltpu.VMEM((held * heads, blk, width), bf),
            pltpu.VMEM((held * heads, blk, width), bf),
            native, native, native,
            pltpu.VMEM((tok, width), f32),
            pltpu.VMEM((tok, width), f32),
            pltpu.VMEM((heads, tok, width), bf),
            pltpu.VMEM((heads, tok, width), bf),
            pltpu.VMEM((heads, tok, 2 * width), bf),
            pltpu.VMEM((heads, CHUNK, width), bf),
            pltpu.VMEM((heads, CHUNK, width), bf),
            pltpu.VMEM((heads, tok, width), bf),
            pltpu.VMEM((heads, tok, 2 * width), f32),
            pltpu.VMEM((heads, tok, width), f32),
            pltpu.VMEM((heads, tok, blk), bf),
            pltpu.VMEM((mem_n + 2, 1, 128), jnp.int32),
            pltpu.SMEM((mem_n + 2, 1, 128), jnp.int32),
            slots, slots, slots, slots,
            dma((5,)), dma((cn,)), dma((cn,)), dma((cn,)), dma((cn,)),
            dma((pieces,)), dma((pieces,)), dma((cn,)), dma((2,)),
            dma, dma, dma((2 * len(PLAN), 4)), dma((2,)), dma, dma, dma,
        ],
        compiler_params=pltpu.CompilerParams(
            collective_id=0, has_side_effects=True, vmem_limit_bytes=56 * 1024 * 1024
        ),
    )(
        queries[0], window_keys[0], window_values[0],
        mem_keys.reshape(held * heads, blk, width), mem_values.reshape(held * heads, blk, width),
        gate_logit, wanted, request,
    )
    return out[None]


def solution(mesh):
    placed = (
        P("dp", ("mem", "ctx"), None, None),
        P("dp", ("mem", "ctx"), None, None),
        P("dp", ("mem", "ctx"), None, None),
        P("mem", None, None, None),
        P("mem", None, None, None),
        P(),
        P("dp", ("mem", "ctx"), None),
    )
    return jax.shard_map(
        local,
        mesh=mesh,
        in_specs=placed,
        out_specs=P("dp", ("mem", "ctx"), None, None),
        check_vma=False,
    )
```

time: 127 us -> 96.2 us (0.76)
  the two profiles are of different devices: /device:TPU:1 before, /device:TPU:16 now
where the time goes in v2:
time: 96.2 us; the launch traced here: 96 us
  Pallas kernels  92.3 us (96%)
  local copies, waits for them, and re-layouts  2.99 us (3%)
    pallas_call x1, Pallas kernels, local(): pl.pallas_call(functools.partial(kernel, (XN, zn, cn, held)), out_shape=j...  92.3 us
    unnamed x1, local copies, waits for them, and re-layouts  2.26 us

profile of v2, /device:TPU:16, one launch (start us, length us, event | category | flops | bytes accessed | tf_op | source)
XLA Modules:
  0.0 96.0 jit_solution(9079952723485583088)
XLA Ops:
  0.0 0.7 and_select_fusion.1
  0.7 0.1 select_reduce_fusion
  0.8 0.7 broadcast_in_dim.26.req_hbm
  1.5 92.3 %shard_map.73 = bf16[128,32,128]{2,1,0:T(8,128)(2,1)} custom-call(bf16[128,32,128]{2,1,0:T(8,128)(2,1)} %bitcast.12, bf16[128,32,128]{2,1,0:T(8,128)(2,1)} %bitcast.13, bf16[128,32,128]{2,1,0:T(8,128)(2,1)} %bitcast.14, bf16[96,64,128]{2,1,0:T(8,128)(2,1)} %bitcast.10, bf16[96,64,128]{2,1,0:T(8,128)(2,1)} %bitcast.11, f32[32]{0:T(128)} %gate_sm.1, ...), custom_call_target="tpu_custom_call" | custom-call | tf_op jit(solution)/shard_map/pallas_call | solution.py:441
  93.8 2.3 %copy.9 = bf16[1,128,32,128]{3,2,1,0:T(8,128)(2,1)} copy(bf16[1,128,32,128]{3,2,1,0:T(8,128)(2,1)} %bitcast.9) | data formatting | bytes 2097152

commit v3 on v2

--- a/solution.py
+++ b/solution.py
@@ -36,12 +36,12 @@
 
 def kernel(
     sizes,
-    q_hbm, k_hbm, v_hbm, mk_hbm, mv_hbm, gate_sm, ids_sm, req_hbm,
+    q_hbm, k_hbm, v_hbm, mk_hbm, mv_hbm, gate_sm, ids_sm, ids_hbm,
     out_hbm,
     q_v, k_v, v_v, mk_v, mv_v,
     qn_v, ansn_v, ansp_v, stn_v, stp_v,
     q_t, k_t, v_t, qn_t, an_t, ap_t, own_o, own_m, mem_w,
-    tab_v, tab_sm, mk_send, mk_recv, mv_send, mv_recv,
+    tab_v, entry_v, tab_sm, mk_send, mk_recv, mv_send, mv_recv,
     load_sem, q_send, q_recv, a_send, a_recv, s_send, s_recv, far_send, far_recv,
     r_send, r_recv, b_send, b_recv, self_sem, tab_sem, out_sem,
 ):
@@ -77,7 +77,7 @@
     ]
     for load in loads:
         load.start()
-    own_row = pltpu.make_async_copy(req_hbm.at[mem], tab_v.at[0], self_sem)
+    own_row = pltpu.make_async_copy(ids_hbm, tab_v.at[0], self_sem)
     own_row.start()
 
     barrier = pltpu.get_barrier_semaphore()
@@ -112,7 +112,7 @@
     def ask(k, _):
         owner = owner_at(k)
         pltpu.make_async_remote_copy(
-            req_hbm.at[owner], tab_v.at[k], r_send, r_recv, (owner, ctx, dp), MESH
+            ids_hbm, tab_v.at[k], r_send, r_recv, (owner, ctx, dp), MESH
         ).start()
         return 0
 
@@ -121,7 +121,7 @@
     def ask_aside(k, j, i):
         owner = owner_at(k)
         return pltpu.make_async_remote_copy(
-            req_hbm.at[owner], tab_v.at[mem_n + i], far_send.at[j], far_recv.at[i], (owner, j, dp), MESH
+            ids_hbm, tab_v.at[mem_n + i], far_send.at[j], far_recv.at[i], (owner, j, dp), MESH
         )
 
     @pl.when(first_ctx)
@@ -181,7 +181,13 @@
     ask_all.wait_recv()
     pl.when(not_first)(lambda: ask_aside(0, 0, 0).wait_recv())
     pl.when(not_last)(lambda: ask_aside(0, 0, 1).wait_recv())
-    to_scalar = pltpu.make_async_copy(tab_v, tab_sm, tab_sem)
+    inside = tab_v[:, 0, :] - mem * held
+    head_of = lax.broadcasted_iota(jnp.int32, inside.shape, 1)
+    entry = jnp.where((inside >= 0) & (inside < held), inside * heads + head_of, 0)
+    entry = jnp.sum(entry, axis=-1, keepdims=True)
+    entry = jnp.clip(entry, 0, held * heads - 1)
+    entry_v[...] = jnp.broadcast_to(entry, entry_v.shape)
+    to_scalar = pltpu.make_async_copy(entry_v, tab_sm, tab_sem)
     to_scalar.start()
     to_scalar.wait()
 
@@ -210,10 +216,10 @@
         if i >= AHEAD:
             batch_done(i - AHEAD)
         if i % batches == 0:
-            recv[0] = held_v[tab_sm[0, 0, 0]]
+            recv[0] = held_v[tab_sm[0, 0]]
 
         def push(k, to, r, there):
-            send[k] = held_v[tab_sm[k, 0, 0]]
+            send[k] = held_v[tab_sm[k, 0]]
             pltpu.make_async_remote_copy(
                 send.at[k], recv.at[to], b_send.at[i, r], b_recv.at[i // batches], there, MESH
             ).start()
@@ -394,9 +400,15 @@
         return 0
 
     some_heads(min(8, heads), recall)
-    by_position(q_v, ap_t, 0, tok)
-    result = pltpu.make_async_copy(q_v, out_hbm, out_sem)
-    result.start()
+
+    def result(c):
+        rows = pl.ds(c * 16, 16)
+        return pltpu.make_async_copy(q_v.at[rows], out_hbm.at[rows], out_sem.at[c])
+
+    for c in range(tok // 16):
+        rows = pl.ds(c * 16, 16)
+        q_v[rows] = jnp.swapaxes(ap_t[:, rows, :], 0, 1)
+        result(c).start()
     ask_all.wait_send()
     for i in range(max(0, 2 * batches - AHEAD), 2 * batches):
         batch_done(i)
@@ -416,7 +428,8 @@
         for j in range(cn - 1):
             ask_aside(UP + j, j, 1).wait_send()
 
-    result.wait()
+    for c in range(tok // 16):
+        result(c).wait()
 
 
 def local(queries, window_keys, window_values, mem_keys, mem_values, gate_logit, block_ids):
@@ -426,12 +439,6 @@
     zn = mem_n // XN
     pieces = tok // CHUNK
     wanted = block_ids[0, 0]
-    head_ids = jnp.arange(heads, dtype=jnp.int32)
-    entry = (wanted % held) * heads + head_ids
-    asked = jnp.where(
-        (wanted // held)[None, :] == jnp.arange(mem_n, dtype=jnp.int32)[:, None], entry[None, :], 0
-    )
-    request = jnp.broadcast_to(jnp.sum(asked, axis=1)[:, None, None], (mem_n, 1, 128))
     anywhere = pl.BlockSpec(memory_space=pl.ANY)
     scalars = pl.BlockSpec(memory_space=pltpu.SMEM)
     bf, f32 = jnp.bfloat16, jnp.float32
@@ -459,12 +466,13 @@
             pltpu.VMEM((heads, tok, 2 * width), f32),
             pltpu.VMEM((heads, tok, width), f32),
             pltpu.VMEM((heads, tok, blk), bf),
-            pltpu.VMEM((mem_n + 2, 1, 128), jnp.int32),
-            pltpu.SMEM((mem_n + 2, 1, 128), jnp.int32),
+            pltpu.VMEM((mem_n + 2, 1, heads), jnp.int32),
+            pltpu.VMEM((mem_n + 2, 128), jnp.int32),
+            pltpu.SMEM((mem_n + 2, 128), jnp.int32),
             slots, slots, slots, slots,
             dma((5,)), dma((cn,)), dma((cn,)), dma((cn,)), dma((cn,)),
             dma((pieces,)), dma((pieces,)), dma((cn,)), dma((2,)),
-            dma, dma, dma((2 * len(PLAN), 4)), dma((2,)), dma, dma, dma,
+            dma, dma, dma((2 * len(PLAN), 4)), dma((2,)), dma, dma, dma((tok // 16,)),
         ],
         compiler_params=pltpu.CompilerParams(
             collective_id=0, has_side_effects=True, vmem_limit_bytes=56 * 1024 * 1024
@@ -472,7 +480,7 @@
     )(
         queries[0], window_keys[0], window_values[0],
         mem_keys.reshape(held * heads, blk, width), mem_values.reshape(held * heads, blk, width),
-        gate_logit, wanted, request,
+        gate_logit, wanted, block_ids[0],
     )
     return out[None]
 

time: 96.2 us -> 95.5 us (level)
  no operation moved by 1% of the time
where the time goes in v3:
time: 95.5 us; the launch traced here: 95.3 us
  Pallas kernels  93 us (97%)
  local copies, waits for them, and re-layouts  2.26 us (2%)
    pallas_call x1, Pallas kernels, local(): pl.pallas_call(functools.partial(kernel, (XN, zn, cn, held)), out_shape=j...  93 us
    unnamed x1, local copies, waits for them, and re-layouts  2.26 us

profile of v3, /device:TPU:16, one launch (start us, length us, event | category | flops | bytes accessed | tf_op | source)
XLA Modules:
  0.0 95.3 jit_solution(11370934908245718715)
XLA Ops:
  0.0 93.0 %shard_map.73 = bf16[128,32,128]{2,1,0:T(8,128)(2,1)} custom-call(bf16[128,32,128]{2,1,0:T(8,128)(2,1)} %bitcast.11, bf16[128,32,128]{2,1,0:T(8,128)(2,1)} %bitcast.12, bf16[128,32,128]{2,1,0:T(8,128)(2,1)} %bitcast.13, bf16[96,64,128]{2,1,0:T(8,128)(2,1)} %bitcast.9, bf16[96,64,128]{2,1,0:T(8,128)(2,1)} %bitcast.10, f32[32]{0:T(128)} %gate_sm.1, ...), custom_call_target="tpu_custom_call" | custom-call | tf_op jit(solution)/shard_map/pallas_call | solution.py:448
  93.1 2.3 %copy.9 = bf16[1,128,32,128]{3,2,1,0:T(8,128)(2,1)} copy(bf16[1,128,32,128]{3,2,1,0:T(8,128)(2,1)} %bitcast.8) | data formatting | bytes 2097152

commit v4 on v3

--- a/solution.py
+++ b/solution.py
@@ -37,13 +37,13 @@
 def kernel(
     sizes,
     q_hbm, k_hbm, v_hbm, mk_hbm, mv_hbm, gate_sm, ids_sm, ids_hbm,
-    out_hbm,
+    out_hbm, near_hbm,
     q_v, k_v, v_v, mk_v, mv_v,
     qn_v, ansn_v, ansp_v, stn_v, stp_v,
     q_t, k_t, v_t, qn_t, an_t, ap_t, own_o, own_m, mem_w,
     tab_v, entry_v, tab_sm, mk_send, mk_recv, mv_send, mv_recv,
     load_sem, q_send, q_recv, a_send, a_recv, s_send, s_recv, far_send, far_recv,
-    r_send, r_recv, b_send, b_recv, self_sem, tab_sem, out_sem,
+    r_send, r_recv, b_send, b_recv, self_sem, tab_sem, out_sem, near_sem,
 ):
     xn, zn, cn, held = sizes
     mem_n = xn * zn
@@ -386,17 +386,26 @@
             mine = own_o[h]
             above = part_p * ap_t[h].astype(jnp.float32) + part_o * mine[:, :width]
             below = part_p * sum_p + part_o * mine[:, width:]
-            own_m[h] = (1.0 - gate_of(h)) * (above / below)
+            ap_t[h] = ((1.0 - gate_of(h)) * (above / below)).astype(jnp.bfloat16)
         return 0
 
     some_heads(UNROLL, join)
+
+    def near(c):
+        rows = pl.ds(c * 16, 16)
+        return pltpu.make_async_copy(k_v.at[rows], near_hbm.at[rows], near_sem.at[c])
+
+    for c in range(tok // 16):
+        rows = pl.ds(c * 16, 16)
+        k_v[rows] = jnp.swapaxes(ap_t[:, rows, :], 0, 1)
+        near(c).start()
 
     fetched(mv_send, mv_recv, 1).wait_recv()
 
     def recall(hs, _):
         found = [dot_nn(mem_w[h], mv_recv[slot_of(h)]) for h in hs]
         for h, x in zip(hs, found):
-            ap_t[h] = (x + own_m[h]).astype(jnp.bfloat16)
+            ap_t[h] = x.astype(jnp.bfloat16)
         return 0
 
     some_heads(min(8, heads), recall)
@@ -429,6 +438,7 @@
             ask_aside(UP + j, j, 1).wait_send()
 
     for c in range(tok // 16):
+        near(c).wait()
         result(c).wait()
 
 
@@ -445,11 +455,11 @@
     dma = pltpu.SemaphoreType.DMA
     native = pltpu.VMEM((tok, heads, width), bf)
     slots = pltpu.VMEM((mem_n + 2, blk, width), bf)
-    out = pl.pallas_call(
+    far_part, near_part = pl.pallas_call(
         functools.partial(kernel, (XN, zn, cn, held)),
-        out_shape=jax.ShapeDtypeStruct((tok, heads, width), bf),
+        out_shape=[jax.ShapeDtypeStruct((tok, heads, width), bf)] * 2,
         in_specs=[anywhere] * 5 + [scalars, scalars, anywhere],
-        out_specs=anywhere,
+        out_specs=[anywhere] * 2,
         scratch_shapes=[
             native, native, native,
             pltpu.VMEM((held * heads, blk, width), bf),
@@ -472,7 +482,7 @@
             slots, slots, slots, slots,
             dma((5,)), dma((cn,)), dma((cn,)), dma((cn,)), dma((cn,)),
             dma((pieces,)), dma((pieces,)), dma((cn,)), dma((2,)),
-            dma, dma, dma((2 * len(PLAN), 4)), dma((2,)), dma, dma, dma((tok // 16,)),
+            dma, dma, dma((2 * len(PLAN), 4)), dma((2,)), dma, dma, dma((tok // 16,)), dma((tok // 16,)),
         ],
         compiler_params=pltpu.CompilerParams(
             collective_id=0, has_side_effects=True, vmem_limit_bytes=56 * 1024 * 1024
@@ -482,7 +492,7 @@
         mem_keys.reshape(held * heads, blk, width), mem_values.reshape(held * heads, blk, width),
         gate_logit, wanted, block_ids[0],
     )
-    return out[None]
+    return (far_part.astype(f32) + near_part.astype(f32)).astype(bf)[None]
 
 
 def solution(mesh):

time: 95.5 us -> 96.1 us (level)
  other arithmetic: 0 us -> 2.79 us
  local copies, waits for them, and re-layouts: 2.26 us -> 0 us
    broadcast_in_dim x0 -> x1, other arithmetic: none -> 2.79 us  [local(): return (far_part.astype(f32) + near_part.astype(f32)).astype(bf)[None]]
    unnamed x1 -> x0, local copies, waits for them, and re-layouts: 2.26 us -> none
where the time goes in v4:
time: 96.1 us; the launch traced here: 95.9 us
  Pallas kernels  93.1 us (97%)
  other arithmetic  2.79 us (3%)
    pallas_call x1, Pallas kernels, local(): pl.pallas_call(functools.partial(kernel, (XN, zn, cn, held)), out_shape=[...  93.1 us
    broadcast_in_dim x1, other arithmetic, local(): return (far_part.astype(f32) + near_part.astype(f32)).astype(bf)[None]  2.79 us

profile of v4, /device:TPU:16, one launch (start us, length us, event | category | flops | bytes accessed | tf_op | source)
XLA Modules:
  0.0 95.9 jit_solution(15699179710979027394)
XLA Ops:
  0.0 93.1 %shard_map.73 = (bf16[128,32,128]{2,1,0:T(8,128)(2,1)}, bf16[128,32,128]{2,1,0:T(8,128)(2,1)}) custom-call(bf16[128,32,128]{2,1,0:T(8,128)(2,1)} %bitcast.11, bf16[128,32,128]{2,1,0:T(8,128)(2,1)} %bitcast.12, bf16[128,32,128]{2,1,0:T(8,128)(2,1)} %bitcast.13, bf16[96,64,128]{2,1,0:T(8,128)(2,1)} %bitcast.9, bf16[96,64,128]{2,1,0:T(8,128)(2,1)} %bitcast.10, ...), custom_call_target="tpu_custom_call" | custom-call | tf_op jit(solution)/shard_map/pallas_call | solution.py:458
  93.1 2.8 %fusion = bf16[1,128,32,128]{3,2,1,0:T(8,128)(2,1)} fusion(bf16[128,32,128]{2,1,0:T(8,128)(2,1)} %get-tuple-element.8, bf16[128,32,128]{2,1,0:T(8,128)(2,1)} %get-tuple-element.7), kind=kLoop, calls=%fused_computation.1 | loop fusion | flops 2097152 | bytes 3145728 | tf_op jit(solution)/shard_map/broadcast_in_dim | solution.py:495
